TPU v7x, 32 devices: a whole 2x2x4 slice. The times are simulated.
32 devices in a mesh: fsdp: 4 (over z), context: 2 (over y), tensor: 4 (over x, core).
Axes of the slice: x: 2, y: 2, z: 4, core: 2. Of those that a mesh axis runs over, the one named last changes fastest.
Arguments:
- patches: bfloat16 [10240, 768], P(('fsdp', 'context')), may hold values from -6 to 6
- out_grad: bfloat16 [10240, 768], P(('fsdp', 'context')), may hold values from -6 to 6
- block_order: int32 [4, 20], P('fsdp'), may hold values from 0 to 19, as said below
- first_gain: float32 [768], replicated, may hold values from 0.25 to 1.75
- first_shift: float32 [768], replicated, may hold values from -2 to 2
- attn_proj: bfloat16 [3, 768, 768], P(None, 'fsdp', 'tensor'), may hold values from -0.21875 to 0.21875
- attn_bias: float32 [2, 768], P(None, 'tensor'), may hold values from -3 to 3
- out_proj: bfloat16 [768, 768], P('tensor', 'fsdp'), may hold values from -0.875 to 0.875
- out_bias: float32 [768], replicated, may hold values from -2 to 2
- second_gain: float32 [768], replicated, may hold values from 0.25 to 1.75
- second_shift: float32 [768], replicated, may hold values from -2 to 2
- up_proj: bfloat16 [768, 3072], P('fsdp', 'tensor'), may hold values from -0.21875 to 0.21875
- up_bias: float32 [3072], P('tensor'), may hold values from -3 to 3
- down_proj: bfloat16 [3072, 768], P('tensor', 'fsdp'), may hold values from -0.109375 to 0.109375
- down_bias: float32 [768], replicated, may hold values from -2 to 2
Outputs:
- result: bfloat16 [10240, 768], P(('fsdp', 'context'))
- patch_grad: float32 [10240, 768], P(('fsdp', 'context'))
- grad_first_gain: float32 [768], replicated
- grad_first_shift: float32 [768], replicated
- grad_attn_proj: float32 [3, 768, 768], P(None, 'fsdp', 'tensor')
- grad_attn_bias: float32 [2, 768], P(None, 'tensor')
- grad_out_proj: float32 [768, 768], P('tensor', 'fsdp')
- grad_out_bias: float32 [768], replicated
- grad_second_gain: float32 [768], replicated
- grad_second_shift: float32 [768], replicated
- grad_up_proj: float32 [768, 3072], P('fsdp', 'tensor')
- grad_up_bias: float32 [3072], P('tensor')
- grad_down_proj: float32 [3072, 768], P('tensor', 'fsdp')
- grad_down_bias: float32 [768], replicated
Inputs may be any that keep to these rules, and one draw needn't show every extreme that they name: `block_order`: each row lists every block number of its group once. In every group, each device of context holds 20 // 2 blocks of every tree, or one more.
All inputs are finite; a program needn't handle non-finite values.
Results may differ from a plain program's by a relative error of at most 0.0098.
Values may be sent and summed in bfloat16 or wider, within the bound.
A program may use at most 128 MiB of HBM per device.

v0:
```python
from functools import partial
import jax
import jax.numpy as jnp
from jax import lax
from jax.sharding import PartitionSpec as P

HEAD_DIM = 64
BLOCK = 128
TRUNK_BLK = 8
BRANCHES = 4
LEAVES = 2
TREE_BLK = 20
epsilon = 1e-05
far_below = -1e30


def layer_norm(values, norm_gain, norm_shift):
    center = values - jnp.mean(values, axis=1, keepdims=True)
    inverse = lax.rsqrt(jnp.mean(center * center, axis=1, keepdims=True) + epsilon)
    normed = center * inverse
    return (normed * norm_gain + norm_shift, normed, inverse)


def norm_back(gradient, normed, inverse, norm_gain):
    scaled = gradient * norm_gain
    return inverse * (
        scaled
        - jnp.mean(scaled, axis=1, keepdims=True)
        - normed * jnp.mean(scaled * normed, axis=1, keepdims=True)
    )


def slot_labels(order_row):
    position = order_row % TREE_BLK
    return (order_row // TREE_BLK, jnp.where(position < TRUNK_BLK, 0, position - TRUNK_BLK + 1))


def spread_rows(values):
    return jnp.broadcast_to(values[:, None], (values.shape[0], BLOCK)).reshape(-1)


def row_labels(labels, first_slot, slot_count):
    return tuple(
        (
            spread_rows(lax.dynamic_slice_in_dim(label_table, first_slot, slot_count))
            for label_table in labels
        )
    )


def visible(query_labels, key_labels):
    query_tree, query_seg = query_labels
    key_tree, key_seg = key_labels
    parent = jnp.where(query_seg > BRANCHES, 1 + (query_seg - BRANCHES - 1) // LEAVES, 0)
    reaches = (
        (key_seg[None, :] == 0)
        | (key_seg[None, :] == query_seg[:, None])
        | (key_seg[None, :] == parent[:, None])
    )
    return (query_tree[:, None] == key_tree[None, :]) & reaches


def head_view(matrix):
    return matrix.reshape(matrix.shape[0], matrix.shape[1] // HEAD_DIM, HEAD_DIM)


def scores_of(query_heads, key_heads):
    return jnp.einsum(
        "qhd,khd->hqk", query_heads, key_heads, preferred_element_type=jnp.float32
    ) * HEAD_DIM ** (-0.5)


def weights_of(scores, log_total, allowed):
    return jnp.where(allowed[None], jnp.exp(scores - log_total[:, :, None]), 0.0)


def score_grads(query_heads, grad_heads, key_heads, value_heads, log_total, row_delta, allowed):
    weights = weights_of(scores_of(query_heads, key_heads), log_total, allowed)
    prob_grad = jnp.einsum(
        "qhd,khd->hqk", grad_heads, value_heads, preferred_element_type=jnp.float32
    )
    return (
        (weights * (prob_grad - row_delta[:, :, None])).astype(jnp.bfloat16),
        weights.astype(jnp.bfloat16),
    )


def shards(
    patches,
    out_grad,
    block_order,
    first_gain,
    first_shift,
    attn_proj,
    attn_bias,
    out_proj,
    out_bias,
    second_gain,
    second_shift,
    up_proj,
    up_bias,
    down_proj,
    down_bias,
):
    attn_full, out_full, up_full, down_full = (
        lax.all_gather(attn_proj, "fsdp", axis=1, tiled=True),
        lax.all_gather(out_proj, "fsdp", axis=1, tiled=True),
        lax.all_gather(up_proj, "fsdp", axis=0, tiled=True),
        lax.all_gather(down_proj, "fsdp", axis=1, tiled=True),
    )
    labels = slot_labels(block_order[0])
    row_count = patches.shape[0]
    own_slots = row_count // BLOCK
    query_labels = row_labels(labels, lax.axis_index("context") * own_slots, own_slots)
    head_width = attn_full.shape[2]
    head_count = head_width // HEAD_DIM
    key_block = 4 * BLOCK
    block_slots = key_block // BLOCK
    score_scale = HEAD_DIM ** (-0.5)
    inputs = patches.astype(jnp.float32)
    first_norm, first_normed, first_inverse = layer_norm(inputs, first_gain, first_shift)
    first_low = first_norm.astype(jnp.bfloat16)
    projected = jnp.einsum("rd,cde->cre", first_low, attn_full, preferred_element_type=jnp.float32)
    queries = (projected[0] + attn_bias[0]).astype(jnp.bfloat16)
    keys_low = projected[1].astype(jnp.bfloat16)
    values_low = (projected[2] + attn_bias[1]).astype(jnp.bfloat16)
    keys_all = lax.all_gather(
        jnp.concatenate([keys_low, values_low], axis=1), "context", axis=0, tiled=True
    )
    block_count = keys_all.shape[0] // key_block
    query_heads = head_view(queries)

    def key_piece(step_index):
        key_slab = lax.dynamic_slice_in_dim(keys_all, step_index * key_block, key_block, 0)
        allowed = visible(query_labels, row_labels(labels, step_index * block_slots, block_slots))
        return (head_view(key_slab[:, :head_width]), head_view(key_slab[:, head_width:]), allowed)

    def total_step(step_index, carried):
        running_top, running_sum = carried
        key_heads, value_heads, allowed = key_piece(step_index)
        masked = jnp.where(allowed[None], scores_of(query_heads, key_heads), far_below)
        new_top = jnp.maximum(running_top, jnp.max(masked, axis=2))
        kept_exp = jnp.where(allowed[None], jnp.exp(masked - new_top[:, :, None]), 0.0)
        return (new_top, running_sum * jnp.exp(running_top - new_top) + jnp.sum(kept_exp, axis=2))

    start_top = jnp.full((head_count, row_count), far_below, jnp.float32)
    running_top, running_sum = lax.fori_loop(
        0, block_count, total_step, (start_top, jnp.zeros((head_count, row_count), jnp.float32))
    )
    log_total = running_top + jnp.log(running_sum)

    def mix_step(step_index, mixed):
        key_heads, value_heads, allowed = key_piece(step_index)
        weights = weights_of(scores_of(query_heads, key_heads), log_total, allowed).astype(
            jnp.bfloat16
        )
        return mixed + jnp.einsum(
            "hqk,khd->qhd", weights, value_heads, preferred_element_type=jnp.float32
        )

    attended = lax.fori_loop(
        0, block_count, mix_step, jnp.zeros((row_count, head_count, HEAD_DIM), jnp.float32)
    )
    attended_low = attended.reshape(row_count, head_width).astype(jnp.bfloat16)
    attn_part = jnp.dot(attended_low, out_full, preferred_element_type=jnp.float32)
    middle = inputs + (lax.psum(attn_part, "tensor") + out_bias)
    second_norm, second_normed, second_inverse = layer_norm(middle, second_gain, second_shift)
    second_low = second_norm.astype(jnp.bfloat16)
    pre_act = jnp.dot(second_low, up_full, preferred_element_type=jnp.float32) + up_bias
    hidden, gelu_back = jax.vjp(partial(jax.nn.gelu, approximate=False), pre_act)
    hidden_low = hidden.astype(jnp.bfloat16)
    mlp_part = jnp.dot(hidden_low, down_full, preferred_element_type=jnp.float32)
    result = (
        middle + (lax.psum(mlp_part.astype(jnp.bfloat16), "tensor").astype(jnp.float32) + down_bias)
    ).astype(jnp.bfloat16)
    top_grad = out_grad.astype(jnp.float32)
    grad_down_bias = jnp.sum(top_grad, axis=0)
    grad_down = jnp.einsum("rf,rd->fd", hidden_low, out_grad, preferred_element_type=jnp.float32)
    hidden_grad = jnp.einsum("rd,fd->rf", out_grad, down_full, preferred_element_type=jnp.float32)
    pre_grad = gelu_back(hidden_grad)[0].astype(jnp.bfloat16)
    grad_up_bias = jnp.sum(pre_grad.astype(jnp.float32), axis=0)
    grad_up = jnp.einsum("rd,rf->df", second_low, pre_grad, preferred_element_type=jnp.float32)
    second_part = jnp.einsum("rf,df->rd", pre_grad, up_full, preferred_element_type=jnp.float32)
    second_grad = lax.psum(second_part, "tensor")
    grad_second_gain = jnp.sum(second_grad * second_normed, axis=0)
    grad_second_shift = jnp.sum(second_grad, axis=0)
    middle_grad = top_grad + norm_back(second_grad, second_normed, second_inverse, second_gain)
    branch_grad = middle_grad.astype(jnp.bfloat16)
    grad_out_bias = jnp.sum(branch_grad.astype(jnp.float32), axis=0)
    grad_out = jnp.einsum(
        "re,rd->ed", attended_low, branch_grad, preferred_element_type=jnp.float32
    )
    attended_grad = jnp.einsum(
        "rd,ed->re", branch_grad, out_full, preferred_element_type=jnp.float32
    ).astype(jnp.bfloat16)
    grad_heads = head_view(attended_grad)

    def delta_step(step_index, row_delta):
        key_heads, value_heads, allowed = key_piece(step_index)
        weights = weights_of(scores_of(query_heads, key_heads), log_total, allowed)
        prob_grad = jnp.einsum(
            "qhd,khd->hqk", grad_heads, value_heads, preferred_element_type=jnp.float32
        )
        return row_delta + jnp.sum(weights * prob_grad, axis=2)

    row_delta = lax.fori_loop(
        0, block_count, delta_step, jnp.zeros((head_count, row_count), jnp.float32)
    )
    query_start = jnp.zeros((row_count, head_count, HEAD_DIM), jnp.float32)

    def back_step(step_index, carried):
        query_acc, key_acc = carried
        key_heads, value_heads, allowed = key_piece(step_index)
        score_low, weights_low = score_grads(
            query_heads, grad_heads, key_heads, value_heads, log_total, row_delta, allowed
        )
        query_acc = query_acc + jnp.einsum(
            "hqk,khd->qhd", score_low, key_heads, preferred_element_type=jnp.float32
        )
        key_part = jnp.einsum(
            "hqk,qhd->khd", score_low, query_heads, preferred_element_type=jnp.float32
        )
        value_part = jnp.einsum(
            "hqk,qhd->khd", weights_low, grad_heads, preferred_element_type=jnp.float32
        )
        joined = jnp.concatenate(
            [key_part.reshape(key_block, head_width), value_part.reshape(key_block, head_width)],
            axis=1,
        )
        return (
            query_acc,
            lax.dynamic_update_slice_in_dim(key_acc, joined, step_index * key_block, 0),
        )

    key_start = jnp.zeros((keys_all.shape[0], 2 * head_width), jnp.float32)
    query_acc, key_acc = lax.fori_loop(0, block_count, back_step, (query_start, key_start))
    key_value_grad = lax.psum_scatter(key_acc, "context", scatter_dimension=0, tiled=True)
    query_grad = (query_acc.reshape(row_count, head_width) * score_scale).astype(jnp.bfloat16)
    key_grad = (key_value_grad[:, :head_width] * score_scale).astype(jnp.bfloat16)
    value_grad = key_value_grad[:, head_width:].astype(jnp.bfloat16)
    stacked = jnp.stack([query_grad, key_grad, value_grad])
    grad_attn_bias = jnp.stack(
        [
            jnp.sum(query_grad.astype(jnp.float32), axis=0),
            jnp.sum(value_grad.astype(jnp.float32), axis=0),
        ]
    )
    grad_attn = jnp.einsum("rd,cre->cde", first_low, stacked, preferred_element_type=jnp.float32)
    first_grad = lax.psum(
        jnp.einsum("cre,cde->rd", stacked, attn_full, preferred_element_type=jnp.float32), "tensor"
    )
    grad_first_gain = jnp.sum(first_grad * first_normed, axis=0)
    grad_first_shift = jnp.sum(first_grad, axis=0)
    patch_grad = middle_grad + norm_back(first_grad, first_normed, first_inverse, first_gain)
    wide_attn, wide_out, wide_up, wide_down = (
        lax.psum_scatter(grad_attn, ("fsdp", "context"), scatter_dimension=1, tiled=True),
        lax.psum_scatter(grad_out, ("fsdp", "context"), scatter_dimension=1, tiled=True),
        lax.psum_scatter(grad_up, ("fsdp", "context"), scatter_dimension=0, tiled=True),
        lax.psum_scatter(grad_down, ("fsdp", "context"), scatter_dimension=1, tiled=True),
    )
    grad_attn, grad_out, grad_up, grad_down = (
        lax.all_gather(wide_attn, "context", axis=1, tiled=True),
        lax.all_gather(wide_out, "context", axis=1, tiled=True),
        lax.all_gather(wide_up, "context", axis=0, tiled=True),
        lax.all_gather(wide_down, "context", axis=1, tiled=True),
    )
    small_grads = lax.psum(
        (
            grad_first_gain,
            grad_first_shift,
            grad_attn_bias,
            grad_out_bias,
            grad_second_gain,
            grad_second_shift,
            grad_up_bias,
            grad_down_bias,
        ),
        ("fsdp", "context"),
    )
    return (
        result,
        patch_grad,
        small_grads[0],
        small_grads[1],
        grad_attn,
        small_grads[2],
        grad_out,
        small_grads[3],
        small_grads[4],
        small_grads[5],
        grad_up,
        small_grads[6],
        grad_down,
        small_grads[7],
    )


def solution(mesh):
    return jax.shard_map(
        shards,
        mesh=mesh,
        in_specs=(
            P(("fsdp", "context"), None),
            P(("fsdp", "context"), None),
            P("fsdp", None),
            P(),
            P(),
            P(None, "fsdp", "tensor"),
            P(None, "tensor"),
            P("tensor", "fsdp"),
            P(),
            P(),
            P(),
            P("fsdp", "tensor"),
            P("tensor"),
            P("tensor", "fsdp"),
            P(),
        ),
        out_specs=(
            P(("fsdp", "context"), None),
            P(("fsdp", "context"), None),
            P(),
            P(),
            P(None, "fsdp", "tensor"),
            P(None, "tensor"),
            P("tensor", "fsdp"),
            P(),
            P(),
            P(),
            P("fsdp", "tensor"),
            P("tensor"),
            P("tensor", "fsdp"),
            P(),
        ),
        check_vma=False,
    )
```

profile of v0, /device:TPU:0, one launch (start us, length us, event | category | flops | bytes accessed | tf_op | source)
XLA Modules:
  0.0 950.3 jit_solution(17451952683291024522)
XLA Ops:
  13.5 31.5 %all_gather.27 = bf16[3,768,192]{2,0,1:T(4,128)(2,1)} all-gather(bf16[3,192,192]{2,0,1:T(4,128)(2,1)S(1)} %copy.39), channel_id=1, replica_groups=mesh['fsdp'=4,'context'=2,'tensor'=4] {'fsdp'}, dimensions={1}, use_global_device_ids=true | all-gather | bytes 1105920 | tf_op jit(solution)/shard_map/all_gather | solution.py:106
  56.9 16.8 %all_gather.29 = bf16[192,768]{0,1:T(8,128)(2,1)} all-gather(bf16[192,192]{0,1:T(8,128)(2,1)} %copy.42), channel_id=1, replica_groups=mesh['fsdp'=4,'context'=2,'tensor'=4] {'fsdp'}, dimensions={1}, use_global_device_ids=true | all-gather | bytes 368640 | tf_op jit(solution)/shard_map/all_gather | solution.py:107
  73.7 11.5 %all-gather.4.cloned.1.call-done = bf16[2560,384]{0,1:T(8,128)(2,1)} async-done(((bf16[1280,384]{0,1:T(8,128)(2,1)}), bf16[2560,384]{0,1:T(8,128)(2,1)}) %all-gather.4.cloned.1.call-update) | async-done | bytes 1966096 | tf_op jit(solution)/shard_map/all_gather | solution.py:127
  85.2 31.9 %while.88 = (s32[]{:T(128)}, f32[3,1280]{1,0:T(4,128)S(1)}, f32[3,1280]{1,0:T(4,128)S(1)}, s32[20]{0:T(128)S(1)}, s32[20]{0:T(128)S(1)}, /*index=5*/bf16[2560,38...) while((s32[]{:T(128)}, f32[3,1280]{1,0:T(4,128)S(1)}, ...), condition=%wide.region_5.6_spmd.clone.clone.clone, body=%wide.region_2.5_spmd.clone.clone.clone.sunk | while | flops 271363072 | bytes 19016176 | solution.py:147
  117.2 40.3 %while.89 = (s32[]{:T(128)}, f32[1280,3,64]{0,2,1:T(8,128)}, bf16[2560,384]{0,1:T(8,128)(2,1)}, s32[20]{0:T(128)S(1)}, s32[20]{0:T(128)S(1)}, /*index=5*/bf16[12...) while((s32[]{:T(128)}, f32[1280,3,64]{0,2,1:T(8,128)}, ...), condition=%wide.region_7.8_spmd.clone.clone.clone, body=%wide.region_6.7_spmd.clone.clone.clone.sunk | while | flops 515629312 | bytes 5003783 | solution.py:161
  120.1 5.0 fusion.202
  127.9 5.2 fusion.202
  136.0 5.2 fusion.202
  144.1 5.2 fusion.202
  152.2 5.2 fusion.202
  159.5 3.7 fusion.123
  164.9 79.7 %all-reduce.6.cloned.1.call-done = f32[1280,768]{1,0:T(8,128)} async-done(((f32[1280,768]{1,0:T(8,128)}), f32[1280,768]{1,0:T(8,128)}) %all-reduce.6.cloned.1.call-update) | async-done | bytes 3932176 | tf_op jit(solution)/shard_map/psum | solution.py:166
  249.9 6.5 convolution_add_fusion
  256.4 13.5 %convert_reduce_fusion.2 = (f32[768]{0:T(1024)}, bf16[1280,768]{1,0:T(8,128)(2,1)S(1)}, f32[1280,768]{1,0:T(8,128)}) fusion(f32[1280,768]{1,0:T(8,128)} %convolution_add_fusion, bf16[1280,768]{1,0:T(8,128)(2,1)S(1)} %copy-done.10, bf16[768,768]{0,1:T(8,128)(2,1)} %all-gather.8.cloned.1.call-done), kind=kOutput, calls=%fused_computation.149 | convolution fusion | flops 1582693632 | bytes 12979200 | tf_op jit(solution)/shard_map/rd,fd->rf/dot_general | solution.py:179
  271.2 3.7 fusion.124
  275.0 3.9 multiply_convert_fusion
  280.3 3.0 convolution_convert_fusion
  283.4 73.0 %all-reduce.10.cloned.1.call-done = f32[1280,768]{1,0:T(8,128)} async-done(((f32[1280,768]{1,0:T(8,128)}), f32[1280,768]{1,0:T(8,128)}) %all-reduce.10.cloned.1.call-update) | async-done | bytes 3932176 | tf_op jit(solution)/shard_map/psum | solution.py:184
  356.4 5.0 multiply_reduce_fusion
  361.4 47.3 %all-reduce.8.cloned.1.call-done = bf16[1280,768]{1,0:T(8,128)(2,1)} async-done(((bf16[1280,768]{1,0:T(8,128)(2,1)}), bf16[1280,768]{1,0:T(8,128)(2,1)}) %all-reduce.8.cloned.1.call-update) | async-done | bytes 1966096 | tf_op jit(solution)/shard_map/psum | solution.py:174
  408.7 5.9 convert_reduce_fusion.3
  417.3 33.9 %while.90 = (s32[]{:T(128)}, f32[3,1280]{1,0:T(4,128)S(1)}, s32[20]{0:T(128)S(1)}, s32[20]{0:T(128)S(1)}, bf16[2560,384]{0,1:T(8,128)(2,1)}, /*index=5*/bf16[128...) while((s32[]{:T(128)}, f32[3,1280]{1,0:T(4,128)S(1)}, ...), condition=%wide.region_17.18_spmd.clone.clone.clone, body=%wide.region_15.17_spmd.clone.clone.clone.sunk | while | flops 517107712 | bytes 19319308 | solution.py:206
  453.5 59.0 %while.91 = (s32[]{:T(128)}, f32[1280,3,64]{0,2,1:T(8,128)S(1)}, f32[2560,384]{0,1:T(8,128)}, bf16[2560,384]{0,1:T(8,128)(2,1)}, s32[20]{0:T(128)S(1)}, /*index=...) while((s32[]{:T(128)}, f32[1280,3,64]{0,2,1:T(8,128)S(1)}, ...), condition=%wide.region_19.20_spmd.clone.clone.clone, body=%wide.region_18.19_spmd.clone.clone.clone.sunk | while | flops 1282597120 | bytes 45109792 | solution.py:236
  459.2 2.9 fusion.223
  471.0 2.9 fusion.223
  482.8 2.9 fusion.223
  494.6 2.9 fusion.223
  506.4 2.9 fusion.223
  513.5 3.9 convolution_bitcast_fusion.3
  517.5 5.1 fusion.125
  522.7 6.4 fusion.116
  529.3 35.4 %reduce-scatter.10.cloned.1.call-done = f32[1280,384]{0,1:T(8,128)} async-done(((f32[2560,384]{0,1:T(8,128)}), f32[1280,384]{0,1:T(8,128)}) %reduce-scatter.10.cloned.1.call-update) | async-done | bytes 1966096 | tf_op jit(solution)/shard_map/reduce_scatter | solution.py:237
  567.6 3.7 convolution_bitcast_fusion.2
  572.9 2.8 fusion.99
  575.6 4.2 copy.52
  579.9 4.6 reshape.1155
  584.6 46.2 %reduce-scatter.18.cloned.1.call-done = f32[96,192]{1,0:T(8,128)} async-done(((f32[768,192]{1,0:T(8,128)}), f32[96,192]{1,0:T(8,128)}) %reduce-scatter.18.cloned.1.call-update) | async-done | bytes 73744
  630.8 5.5 all_gather.33
  637.1 65.3 %reduce-scatter.14.cloned.1.call-done = f32[768,96]{0,1:T(8,128)} async-done(((f32[768,768]{0,1:T(8,128)}), f32[768,96]{0,1:T(8,128)}) %reduce-scatter.14.cloned.1.call-update) | async-done | bytes 294928 | tf_op jit(solution)/shard_map/reduce_scatter | solution.py:259
  702.4 8.6 all_gather.35
  711.0 63.1 %reduce-scatter.12.cloned.1.call-done = f32[96,768]{1,0:T(8,128)} async-done(((f32[768,768]{1,0:T(8,128)}), f32[96,768]{1,0:T(8,128)}) %reduce-scatter.12.cloned.1.call-update) | async-done | bytes 294928 | tf_op jit(solution)/shard_map/reduce_scatter | solution.py:258
  774.1 9.6 %all_gather.34 = f32[192,768]{1,0:T(8,128)} all-gather(f32[96,768]{1,0:T(8,128)} %reduce-scatter.12.cloned.1.call-done), channel_id=1, replica_groups=mesh['fsdp'=4,'context'=2,'tensor'=4] {'context'}, dimensions={0}, use_global_device_ids=true | all-gather | bytes 884736 | tf_op jit(solution)/shard_map/all_gather | solution.py:264
  783.8 73.6 %all-reduce.12.cloned.1.call-done = f32[1280,768]{1,0:T(8,128)} async-done(((f32[1280,768]{1,0:T(8,128)}), f32[1280,768]{1,0:T(8,128)}) %all-reduce.12.cloned.1.call-update) | async-done | bytes 3932176 | tf_op jit(solution)/shard_map/psum | solution.py:249
  857.4 3.5 fusion.89
  860.9 38.0 %all-reduce = (f32[768]{0:T(1024)}, f32[768]{0:T(1024)}, f32[2,192]{1,0:T(2,128)}, f32[768]{0:T(1024)}, f32[768]{0:T(1024)}, /*index=5*/f32[768]{0:T(1024)}, f32[768]{0:T(1024)}, f32[768]{0:T(1024)}) all-reduce(f32[768]{0:T(1024)S(1)} %get-tuple-element.1970, ...), channel_id=1, replica_groups=mesh['fsdp'=4,'context'=2,'tensor'=4] {'fsdp','context'}, use_global_device_ids=true, to_apply=%region_25.26 | all-reduce | flops 5760 | bytes 46080 | tf_op jit(solution)/shard_map/psum | solution.py:267
  899.0 5.4 fusion.88
  904.3 23.6 %reduce-scatter.16.cloned.1.call-done = f32[96,576]{1,0:T(8,128)} async-done(((f32[768,576]{1,0:T(8,128)}), f32[96,576]{1,0:T(8,128)}) %reduce-scatter.16.cloned.1.call-update) | async-done | bytes 221200
  929.0 9.8 %all_gather.32 = f32[3,192,192]{2,0,1:T(4,128)S(1)} all-gather(f32[3,96,192]{2,0,1:T(4,128)S(1)} %bitcast.417), channel_id=1, replica_groups=mesh['fsdp'=4,'context'=2,'tensor'=4] {'context'}, dimensions={1}, use_global_device_ids=true | all-gather | bytes 663552 | tf_op jit(solution)/shard_map/all_gather | solution.py:262
  (366 shorter events, 168.9 us)
Async XLA Ops:
  8.0 5.2 copy-start.13
  8.0 77.2 %all-gather.4.cloned.1.call-start = ((), (), s32[]{:S(2)}) async-start(), calls=%async_computation.5 | async-start | bytes 2949120 | tf_op jit(solution)/shard_map/all_gather | solution.py:127
  10.7 36.9 %copy-start.2 = (bf16[1280,768]{1,0:T(8,128)(2,1)S(1)}, bf16[1280,768]{1,0:T(8,128)(2,1)}, u32[]{:S(2)}) copy-start(bf16[1280,768]{1,0:T(8,128)(2,1)} %param.23) | copy-start | bytes 5898244
  10.7 36.9 %copy-start.18 = (f32[768]{0:T(1024)S(1)}, f32[768]{0:T(1024)}, u32[]{:S(2)}) copy-start(f32[768]{0:T(1024)} %param.26) | copy-start | bytes 9220
  10.7 36.9 %copy-start.31 = (f32[768]{0:T(1024)S(1)}, f32[768]{0:T(1024)}, u32[]{:S(2)}) copy-start(f32[768]{0:T(1024)} %param.27) | copy-start | bytes 9220
  10.8 38.4 %copy-start.14 = (f32[1280]{0:T(1024)}, f32[1280]{0:T(1024)S(1)}, u32[]{:S(2)}) copy-start(f32[1280]{0:T(1024)S(1)} %broadcast_multiply_fusion.5) | copy-start | bytes 15364
  13.2 36.0 %copy-start.16 = (f32[1280]{0:T(1024)}, f32[1280]{0:T(1024)S(1)}, u32[]{:S(2)}) copy-start(f32[1280]{0:T(1024)S(1)} %add_rsqrt_fusion.1) | copy-start | bytes 15364
  47.6 1.6 copy-start.11
  49.2 1.6 copy-start.7
  49.2 4.2 copy-start.33
  52.0 192.6 %all-reduce.6.cloned.1.call-start = ((), (), s32[]{:S(2)}) async-start(), calls=%async_computation.6 | async-start | bytes 7864320 | tf_op jit(solution)/shard_map/psum | solution.py:166
  158.7 0.8 copy-start.4
  159.5 85.1 %copy-start.23 = (f32[768]{0:T(1024)S(1)}, f32[768]{0:T(1024)}, u32[]{:S(2)}) copy-start(f32[768]{0:T(1024)} %param.31) | copy-start | bytes 9220
  163.2 86.7 %all-gather.6.cloned.1.call-start = ((), (), s32[]{:S(2)}) async-start(), calls=%async_computation.7 | async-start | bytes 1474560 | tf_op jit(solution)/shard_map/all_gather | solution.py:108
  163.8 92.7 %all-gather.8.cloned.1.call-start = ((), (), s32[]{:S(2)}) async-start(), calls=%async_computation.8 | async-start | bytes 1474560 | tf_op jit(solution)/shard_map/all_gather | solution.py:109
  164.4 192.1 %all-reduce.10.cloned.1.call-start = ((), (), s32[]{:S(2)}) async-start(), calls=%async_computation.10 | async-start | bytes 7864320 | tf_op jit(solution)/shard_map/psum | solution.py:184
  247.3 1.9 copy-start.1
  247.3 2.6 copy-start.20
  247.3 2.6 copy-start.28
  247.3 2.6 copy-start.29
  249.8 6.6 copy-start.10
  256.4 14.8 %copy-start.27 = (bf16[768,768]{1,0:T(8,128)(2,1)S(1)}, bf16[768,768]{1,0:T(8,128)(2,1)}, u32[]{:S(2)}) copy-start(bf16[768,768]{1,0:T(8,128)(2,1)} %all-gather.6.cloned.1.call-done) | copy-start | bytes 3538948
  269.9 1.3 copy-start.34
  274.9 133.8 %all-reduce.8.cloned.1.call-start = ((), (), s32[]{:S(2)}) async-start(), calls=%async_computation.9 | async-start | bytes 3932160 | tf_op jit(solution)/shard_map/psum | solution.py:174
  275.0 5.3 copy-start.26
  278.9 1.4 copy-start.8
  283.3 281.4 %reduce-scatter.10.cloned.1.call-start = ((), (), s32[]{:S(2)}) async-start(), calls=%async_computation.11 | async-start | bytes 5898240 | tf_op jit(solution)/shard_map/reduce_scatter | solution.py:237
  283.4 125.3 %copy-start.24 = (f32[768]{0:T(1024)S(1)}, f32[768]{0:T(1024)}, u32[]{:S(2)}) copy-start(f32[768]{0:T(1024)} %param.37) | copy-start | bytes 9220
  408.7 7.8 copy-start.6
  414.6 1.9 copy-start
  512.5 1.0 copy-start.5
  512.5 5.0 copy-start.9
  512.5 118.2 %reduce-scatter.18.cloned.1.call-start = ((), (), s32[]{:S(2)}) async-start(), calls=%async_computation.16 | async-start | bytes 884736
  517.4 5.3 copy-start.30
  517.5 184.9 %reduce-scatter.14.cloned.1.call-start = ((), (), s32[]{:S(2)}) async-start(), calls=%async_computation.14 | async-start | bytes 2654208 | tf_op jit(solution)/shard_map/reduce_scatter | solution.py:259
  522.7 251.5 %reduce-scatter.12.cloned.1.call-start = ((), (), s32[]{:S(2)}) async-start(), calls=%async_computation.13 | async-start | bytes 2654208 | tf_op jit(solution)/shard_map/reduce_scatter | solution.py:258
  529.1 38.5 %copy-start.12 = (bf16[3,768,192]{1,2,0:T(8,128)(2,1)S(1)}, bf16[3,768,192]{1,2,0:T(8,128)(2,1)}, u32[]{:S(2)}) copy-start(bf16[3,768,192]{1,2,0:T(8,128)(2,1)} %copy-done.11) | copy-start | bytes 2654212
  529.1 328.2 %all-reduce.12.cloned.1.call-start = ((), (), s32[]{:S(2)}) async-start(), calls=%async_computation.12 | async-start | bytes 7864320 | tf_op jit(solution)/shard_map/psum | solution.py:249
  571.3 1.5 copy-start.3
  571.3 1.5 copy-start.15
  571.3 1.5 copy-start.17
  571.3 1.5 copy-start.19
  571.3 1.5 copy-start.32
  571.3 356.5 %reduce-scatter.16.cloned.1.call-start = ((), (), s32[]{:S(2)}) async-start(), calls=%async_computation.15 | async-start | bytes 2211840
  637.1 223.8 %copy-start.21 = (f32[768]{0:T(1024)S(1)}, f32[768]{0:T(1024)}, u32[]{:S(2)}) copy-start(f32[768]{0:T(1024)} %get-tuple-element.1968) | copy-start | bytes 9220
  637.1 223.8 %copy-start.22 = (f32[768]{0:T(1024)S(1)}, f32[768]{0:T(1024)}, u32[]{:S(2)}) copy-start(f32[768]{0:T(1024)} %get-tuple-element.1974) | copy-start | bytes 9220
  637.1 223.9 %copy-start.25 = (f32[768]{0:T(1024)S(1)}, f32[768]{0:T(1024)}, u32[]{:S(2)}) copy-start(f32[768]{0:T(1024)} %get-tuple-element.2064) | copy-start | bytes 9220
Sparse Core Ops, SparseCore 0:
  52.1 33.0 all-gather.3
  163.3 81.2 all-reduce.5
  275.0 81.3 all-reduce.9
  359.2 49.3 all-reduce.7
  512.6 52.0 reduce-scatter.9
  568.3 62.4 reduce-scatter.17
  634.3 68.0 reduce-scatter.13
  705.9 68.1 reduce-scatter.11
  777.1 80.2 all-reduce.11
  860.7 67.1 reduce-scatter.15
Sparse Core Ops, SparseCore 1:
  165.2 30.2 all-gather.5
  196.9 29.4 all-gather.7
where the time goes:
time: 960 us; the launch traced here: 950 us
  waiting for transfers between devices  520 us (54%)
  matrix products  149 us (16%)
  blocking collectives  120 us (12%)
  other arithmetic  79.5 us (8%)
  local copies, waits for them, and re-layouts  63.7 us (7%)
  between operations  16.6 us (2%)
    psum x1, waiting for transfers between devices, shards(): middle = inputs + (lax.psum(attn_part, 'tensor') + out_bias)  79.7 us
    psum x1, waiting for transfers between devices, shards(): lax.psum(jnp.einsum('cre,cde->rd', stacked, attn_full, preferred_element_...  73.6 us
    psum x1, waiting for transfers between devices, shards(): second_grad = lax.psum(second_part, 'tensor')  73 us
    unnamed x14, waiting for transfers between devices  70.9 us
    reduce_scatter x1, waiting for transfers between devices, shards(): lax.psum_scatter(grad_down, ('fsdp', 'context'), scatter_dimension=1, til...  65.3 us
    reduce_scatter x1, waiting for transfers between devices, shards(): lax.psum_scatter(grad_up, ('fsdp', 'context'), scatter_dimension=0, tiled...  63.1 us
    psum x1, waiting for transfers between devices, shards(): lax.psum(mlp_part.astype(jnp.bfloat16), 'tensor').astype(jnp.float32)  47.3 us
    psum x1, blocking collectives, shards(): lax.psum((grad_first_gain, grad_first_shift, grad_attn_bias, grad_out_bia...  38 us
  transfers between devices with their start and end apart: 12, of which 10 were waited for; matrix products, arithmetic and copies ran while one was open for 7% of the time, Pallas kernels for 0%

commit v1 on v0

--- a/solution.py
+++ b/solution.py
@@ -246,8 +246,12 @@
         ]
     )
     grad_attn = jnp.einsum("rd,cre->cde", first_low, stacked, preferred_element_type=jnp.float32)
-    first_grad = lax.psum(
-        jnp.einsum("cre,cde->rd", stacked, attn_full, preferred_element_type=jnp.float32), "tensor"
+    first_grad = jnp.sum(
+        lax.all_gather(
+            jnp.einsum("cre,cde->rd", stacked, attn_full, preferred_element_type=jnp.float32),
+            "tensor",
+        ),
+        axis=0,
     )
     grad_first_gain = jnp.sum(first_grad * first_normed, axis=0)
     grad_first_shift = jnp.sum(first_grad, axis=0)

time: 960 us -> 1030 us (1.073)
  waiting for transfers between devices: 520 us -> 571 us
  other arithmetic: 79.5 us -> 94.3 us
    all_gather x0 -> x1, waiting for transfers between devices: none -> 88.8 us  [shards(): lax.all_gather(jnp.einsum('cre,cde->rd', stacked, attn_full, preferred_el...]
    psum x1 -> x0, waiting for transfers between devices: 73.6 us -> none  [shards(): lax.psum(jnp.einsum('cre,cde->rd', stacked, attn_full, preferred_element_...]
    unnamed x14, waiting for transfers between devices: 70.9 us -> 107 us
    reduce_sum x0 -> x2, other arithmetic: none -> 15.3 us  [the longest x1 8.92 us: shards(): jnp.sum(lax.all_gather(jnp.einsum('cre,cde->rd', stacked, attn_full, pref...]
    unnamed x80 -> x92, local copies, waits for them, and re-layouts: 28.8 us -> 27.1 us
  transfers between devices with their start and end apart: 12 -> 12, of which waited for: 10 -> 10; matrix products, arithmetic and copies ran while one was open for 7% -> 6% of each run, Pallas kernels for 0% -> 0%
where the time goes in v1:
time: 1030 us; the launch traced here: 1020 us
  waiting for transfers between devices  571 us (55%)
  matrix products  150 us (15%)
  blocking collectives  120 us (12%)
  other arithmetic  94.3 us (9%)
  local copies, waits for them, and re-layouts  62.1 us (6%)
  between operations  16.5 us (2%)
    unnamed x14, waiting for transfers between devices  107 us
    all_gather x1, waiting for transfers between devices, shards(): lax.all_gather(jnp.einsum('cre,cde->rd', stacked, attn_full, preferred_el...  88.8 us
    psum x1, waiting for transfers between devices, shards(): middle = inputs + (lax.psum(attn_part, 'tensor') + out_bias)  80 us
    psum x1, waiting for transfers between devices, shards(): second_grad = lax.psum(second_part, 'tensor')  73.1 us
    reduce_scatter x1, waiting for transfers between devices, shards(): lax.psum_scatter(grad_down, ('fsdp', 'context'), scatter_dimension=1, til...  65.4 us
    reduce_scatter x1, waiting for transfers between devices, shards(): lax.psum_scatter(grad_up, ('fsdp', 'context'), scatter_dimension=0, tiled...  63.1 us
    psum x1, waiting for transfers between devices, shards(): lax.psum(mlp_part.astype(jnp.bfloat16), 'tensor').astype(jnp.float32)  47.2 us
    psum x1, blocking collectives, shards(): lax.psum((grad_first_gain, grad_first_shift, grad_attn_bias, grad_out_bia...  37.7 us
  transfers between devices with their start and end apart: 12, of which 10 were waited for; matrix products, arithmetic and copies ran while one was open for 6% of the time, Pallas kernels for 0%

profile of v1, /device:TPU:0, one launch (start us, length us, event | category | flops | bytes accessed | tf_op | source)
XLA Modules:
  0.0 1015.5 jit_solution(12448731424534735921)
XLA Ops:
  13.5 31.5 %all_gather.33 = bf16[3,768,192]{2,0,1:T(4,128)(2,1)} all-gather(bf16[3,192,192]{2,0,1:T(4,128)(2,1)S(1)} %copy.39), channel_id=1, replica_groups=mesh['fsdp'=4,'context'=2,'tensor'=4] {'fsdp'}, dimensions={1}, use_global_device_ids=true | all-gather | bytes 1105920 | tf_op jit(solution)/shard_map/all_gather | solution.py:106
  56.9 16.8 %all_gather.35 = bf16[192,768]{0,1:T(8,128)(2,1)} all-gather(bf16[192,192]{0,1:T(8,128)(2,1)} %copy.42), channel_id=1, replica_groups=mesh['fsdp'=4,'context'=2,'tensor'=4] {'fsdp'}, dimensions={1}, use_global_device_ids=true | all-gather | bytes 368640 | tf_op jit(solution)/shard_map/all_gather | solution.py:107
  73.8 11.5 %all-gather.6.cloned.1.call-done = bf16[2560,384]{0,1:T(8,128)(2,1)} async-done(((bf16[1280,384]{0,1:T(8,128)(2,1)}), bf16[2560,384]{0,1:T(8,128)(2,1)}) %all-gather.6.cloned.1.call-update) | async-done | bytes 1966096 | tf_op jit(solution)/shard_map/all_gather | solution.py:127
  85.2 31.9 %while.88 = (s32[]{:T(128)}, f32[3,1280]{1,0:T(4,128)S(1)}, f32[3,1280]{1,0:T(4,128)S(1)}, s32[20]{0:T(128)S(1)}, s32[20]{0:T(128)S(1)}, /*index=5*/bf16[2560,38...) while((s32[]{:T(128)}, f32[3,1280]{1,0:T(4,128)S(1)}, ...), condition=%wide.region_5.6_spmd.clone.clone.clone, body=%wide.region_2.5_spmd.clone.clone.clone.sunk | while | flops 271363072 | bytes 19016176 | solution.py:147
  117.2 40.2 %while.89 = (s32[]{:T(128)}, f32[1280,3,64]{0,2,1:T(8,128)}, bf16[2560,384]{0,1:T(8,128)(2,1)}, s32[20]{0:T(128)S(1)}, s32[20]{0:T(128)S(1)}, /*index=5*/bf16[12...) while((s32[]{:T(128)}, f32[1280,3,64]{0,2,1:T(8,128)}, ...), condition=%wide.region_7.8_spmd.clone.clone.clone, body=%wide.region_6.7_spmd.clone.clone.clone.sunk | while | flops 515629312 | bytes 5003783 | solution.py:161
  120.1 5.0 fusion.202
  127.9 5.2 fusion.202
  136.0 5.2 fusion.202
  144.1 5.2 fusion.202
  152.2 5.2 fusion.202
  159.4 3.7 fusion.123
  164.5 80.0 %all-reduce.5.cloned.1.call-done = f32[1280,768]{1,0:T(8,128)} async-done(((f32[1280,768]{1,0:T(8,128)}), f32[1280,768]{1,0:T(8,128)}) %all-reduce.5.cloned.1.call-update) | async-done | bytes 3932176 | tf_op jit(solution)/shard_map/psum | solution.py:166
  249.8 6.5 convolution_add_fusion
  256.4 13.5 %convert_reduce_fusion.2 = (f32[768]{0:T(1024)}, bf16[1280,768]{1,0:T(8,128)(2,1)S(1)}, f32[1280,768]{1,0:T(8,128)}) fusion(f32[1280,768]{1,0:T(8,128)} %convolution_add_fusion, bf16[1280,768]{1,0:T(8,128)(2,1)S(1)} %copy-done.12, bf16[768,768]{0,1:T(8,128)(2,1)} %all-gather.10.cloned.1.call-done), kind=kOutput, calls=%fused_computation.149 | convolution fusion | flops 1582693632 | bytes 12979200 | tf_op jit(solution)/shard_map/rd,fd->rf/dot_general | solution.py:179
  271.2 3.7 fusion.124
  275.0 3.9 multiply_convert_fusion
  280.2 3.0 convolution_convert_fusion
  283.4 73.1 %all-reduce.9.cloned.1.call-done = f32[1280,768]{1,0:T(8,128)} async-done(((f32[1280,768]{1,0:T(8,128)}), f32[1280,768]{1,0:T(8,128)}) %all-reduce.9.cloned.1.call-update) | async-done | bytes 3932176 | tf_op jit(solution)/shard_map/psum | solution.py:184
  356.4 5.0 multiply_reduce_fusion
  361.4 47.2 %all-reduce.7.cloned.1.call-done = bf16[1280,768]{1,0:T(8,128)(2,1)} async-done(((bf16[1280,768]{1,0:T(8,128)(2,1)}), bf16[1280,768]{1,0:T(8,128)(2,1)}) %all-reduce.7.cloned.1.call-update) | async-done | bytes 1966096 | tf_op jit(solution)/shard_map/psum | solution.py:174
  408.7 6.5 convert_reduce_fusion.3
  417.9 33.9 %while.90 = (s32[]{:T(128)}, f32[3,1280]{1,0:T(4,128)S(1)}, s32[20]{0:T(128)S(1)}, s32[20]{0:T(128)S(1)}, bf16[2560,384]{0,1:T(8,128)(2,1)}, /*index=5*/bf16[128...) while((s32[]{:T(128)}, f32[3,1280]{1,0:T(4,128)S(1)}, ...), condition=%wide.region_17.18_spmd.clone.clone.clone, body=%wide.region_15.17_spmd.clone.clone.clone.sunk | while | flops 517107712 | bytes 19319308 | solution.py:206
  454.1 59.0 %while.91 = (s32[]{:T(128)}, f32[1280,3,64]{0,2,1:T(8,128)S(1)}, f32[2560,384]{0,1:T(8,128)}, bf16[2560,384]{0,1:T(8,128)(2,1)}, s32[20]{0:T(128)S(1)}, /*index=...) while((s32[]{:T(128)}, f32[1280,3,64]{0,2,1:T(8,128)S(1)}, ...), condition=%wide.region_19.20_spmd.clone.clone.clone, body=%wide.region_18.19_spmd.clone.clone.clone.sunk | while | flops 1282597120 | bytes 45109792 | solution.py:236
  459.8 2.9 fusion.223
  471.7 2.9 fusion.223
  495.3 2.9 fusion.223
  507.1 2.9 fusion.223
  514.1 3.9 convolution_bitcast_fusion.3
  518.1 5.2 fusion.125
  523.4 6.3 fusion.116
  529.9 35.4 %reduce-scatter.10.cloned.1.call-done = f32[1280,384]{0,1:T(8,128)} async-done(((f32[2560,384]{0,1:T(8,128)}), f32[1280,384]{0,1:T(8,128)}) %reduce-scatter.10.cloned.1.call-update) | async-done | bytes 1966096 | tf_op jit(solution)/shard_map/reduce_scatter | solution.py:237
  572.1 4.2 copy.52
  576.3 4.7 reshape.1156
  581.1 4.8 convolution_bitcast_fusion.2
  586.0 45.4 %reduce-scatter.18.cloned.1.call-done = f32[96,192]{1,0:T(8,128)} async-done(((f32[768,192]{1,0:T(8,128)}), f32[96,192]{1,0:T(8,128)}) %reduce-scatter.18.cloned.1.call-update) | async-done | bytes 73744
  631.4 5.5 all_gather.41
  637.7 65.4 %reduce-scatter.14.cloned.1.call-done = f32[768,96]{0,1:T(8,128)} async-done(((f32[768,768]{0,1:T(8,128)}), f32[768,96]{0,1:T(8,128)}) %reduce-scatter.14.cloned.1.call-update) | async-done | bytes 294928 | tf_op jit(solution)/shard_map/reduce_scatter | solution.py:263
  703.1 8.6 all_gather.43
  711.7 63.1 %reduce-scatter.12.cloned.1.call-done = f32[96,768]{1,0:T(8,128)} async-done(((f32[768,768]{1,0:T(8,128)}), f32[96,768]{1,0:T(8,128)}) %reduce-scatter.12.cloned.1.call-update) | async-done | bytes 294928 | tf_op jit(solution)/shard_map/reduce_scatter | solution.py:262
  774.8 9.6 all_gather.42
  784.4 60.0 %reduce-scatter.16.cloned.1.call-done = f32[96,576]{1,0:T(8,128)} async-done(((f32[768,576]{1,0:T(8,128)}), f32[96,576]{1,0:T(8,128)}) %reduce-scatter.16.cloned.1.call-update) | async-done | bytes 221200
  845.5 10.1 all_gather.40
  856.6 88.8 %all-gather.12.cloned.1.call-done = f32[5120,768]{1,0:T(8,128)} async-done(((f32[1280,768]{1,0:T(8,128)}), f32[5120,768]{1,0:T(8,128)}) %all-gather.12.cloned.1.call-update) | async-done | bytes 15728656 | tf_op jit(solution)/shard_map/all_gather | solution.py:250
  945.3 8.9 reduce_sum.208
  954.3 3.5 fusion.89
  957.8 4.3 fusion.88
  962.2 6.4 reduce_sum.212
  968.6 37.7 %all-reduce = (f32[768]{0:T(1024)}, f32[768]{0:T(1024)}, f32[2,192]{1,0:T(2,128)}, f32[768]{0:T(1024)}, f32[768]{0:T(1024)}, /*index=5*/f32[768]{0:T(1024)}, f32[768]{0:T(1024)}, f32[768]{0:T(1024)}) all-reduce(f32[768]{0:T(1024)S(1)} %get-tuple-element.1970, ...), channel_id=1, replica_groups=mesh['fsdp'=4,'context'=2,'tensor'=4] {'fsdp','context'}, use_global_device_ids=true, to_apply=%region_25.26 | all-reduce | flops 5760 | bytes 46080 | tf_op jit(solution)/shard_map/psum | solution.py:271
  (380 shorter events, 172.8 us)
Async XLA Ops:
  8.0 5.2 copy-start.17
  8.0 77.2 %all-gather.6.cloned.1.call-start = ((), (), s32[]{:S(2)}) async-start(), calls=%async_computation.5 | async-start | bytes 2949120 | tf_op jit(solution)/shard_map/all_gather | solution.py:127
  10.7 36.9 %copy-start.3 = (bf16[1280,768]{1,0:T(8,128)(2,1)S(1)}, bf16[1280,768]{1,0:T(8,128)(2,1)}, u32[]{:S(2)}) copy-start(bf16[1280,768]{1,0:T(8,128)(2,1)} %param.23) | copy-start | bytes 5898244
  10.7 36.9 %copy-start.22 = (f32[768]{0:T(1024)S(1)}, f32[768]{0:T(1024)}, u32[]{:S(2)}) copy-start(f32[768]{0:T(1024)} %param.26) | copy-start | bytes 9220
  10.7 36.9 %copy-start.37 = (f32[768]{0:T(1024)S(1)}, f32[768]{0:T(1024)}, u32[]{:S(2)}) copy-start(f32[768]{0:T(1024)} %param.27) | copy-start | bytes 9220
  10.8 38.4 %copy-start.18 = (f32[1280]{0:T(1024)}, f32[1280]{0:T(1024)S(1)}, u32[]{:S(2)}) copy-start(f32[1280]{0:T(1024)S(1)} %broadcast_multiply_fusion.5) | copy-start | bytes 15364
  13.2 36.0 %copy-start.20 = (f32[1280]{0:T(1024)}, f32[1280]{0:T(1024)S(1)}, u32[]{:S(2)}) copy-start(f32[1280]{0:T(1024)S(1)} %add_rsqrt_fusion.1) | copy-start | bytes 15364
  47.6 1.6 copy-start.13
  49.2 1.6 copy-start.9
  49.2 4.2 copy-start.39
  52.0 192.5 %all-reduce.5.cloned.1.call-start = ((), (), s32[]{:S(2)}) async-start(), calls=%async_computation.6 | async-start | bytes 7864320 | tf_op jit(solution)/shard_map/psum | solution.py:166
  159.4 85.1 %copy-start.29 = (f32[768]{0:T(1024)S(1)}, f32[768]{0:T(1024)}, u32[]{:S(2)}) copy-start(f32[768]{0:T(1024)} %param.31) | copy-start | bytes 9220
  163.1 86.7 %all-gather.8.cloned.1.call-start = ((), (), s32[]{:S(2)}) async-start(), calls=%async_computation.7 | async-start | bytes 1474560 | tf_op jit(solution)/shard_map/all_gather | solution.py:108
  163.7 92.6 %all-gather.10.cloned.1.call-start = ((), (), s32[]{:S(2)}) async-start(), calls=%async_computation.8 | async-start | bytes 1474560 | tf_op jit(solution)/shard_map/all_gather | solution.py:109
  164.3 192.1 %all-reduce.9.cloned.1.call-start = ((), (), s32[]{:S(2)}) async-start(), calls=%async_computation.10 | async-start | bytes 7864320 | tf_op jit(solution)/shard_map/psum | solution.py:184
  247.2 1.9 copy-start.2
  247.2 2.6 copy-start.24
  247.2 2.6 copy-start.34
  247.3 2.6 copy-start.35
  249.7 6.6 copy-start.12
  256.4 14.9 %copy-start.33 = (bf16[768,768]{1,0:T(8,128)(2,1)S(1)}, bf16[768,768]{1,0:T(8,128)(2,1)}, u32[]{:S(2)}) copy-start(bf16[768,768]{1,0:T(8,128)(2,1)} %all-gather.8.cloned.1.call-done) | copy-start | bytes 3538948
  274.9 133.8 %all-reduce.7.cloned.1.call-start = ((), (), s32[]{:S(2)}) async-start(), calls=%async_computation.9 | async-start | bytes 3932160 | tf_op jit(solution)/shard_map/psum | solution.py:174
  274.9 5.3 copy-start.32
  283.3 282.1 %reduce-scatter.10.cloned.1.call-start = ((), (), s32[]{:S(2)}) async-start(), calls=%async_computation.11 | async-start | bytes 5898240 | tf_op jit(solution)/shard_map/reduce_scatter | solution.py:237
  283.4 125.3 %copy-start.30 = (f32[768]{0:T(1024)S(1)}, f32[768]{0:T(1024)}, u32[]{:S(2)}) copy-start(f32[768]{0:T(1024)} %param.37) | copy-start | bytes 9220
  408.7 8.4 copy-start.7
  415.2 1.9 copy-start
  513.1 5.0 copy-start.11
  513.1 118.3 %reduce-scatter.18.cloned.1.call-start = ((), (), s32[]{:S(2)}) async-start(), calls=%async_computation.16 | async-start | bytes 884736
  518.1 5.3 copy-start.36
  518.1 185.0 %reduce-scatter.14.cloned.1.call-start = ((), (), s32[]{:S(2)}) async-start(), calls=%async_computation.13 | async-start | bytes 2654208 | tf_op jit(solution)/shard_map/reduce_scatter | solution.py:263
  523.3 251.5 %reduce-scatter.12.cloned.1.call-start = ((), (), s32[]{:S(2)}) async-start(), calls=%async_computation.12 | async-start | bytes 2654208 | tf_op jit(solution)/shard_map/reduce_scatter | solution.py:262
  529.7 39.5 %copy-start.4 = (bf16[1280,768]{1,0:T(8,128)(2,1)S(1)}, bf16[1280,768]{1,0:T(8,128)(2,1)}, u32[]{:S(2)}) copy-start(bf16[1280,768]{1,0:T(8,128)(2,1)} %param.23) | copy-start | bytes 5898244
  529.7 39.5 %copy-start.19 = (f32[1280]{0:T(1024)S(1)}, f32[1280]{0:T(1024)}, u32[]{:S(2)}) copy-start(f32[1280]{0:T(1024)} %copy-done.18) | copy-start | bytes 15364
  529.7 39.5 %copy-start.21 = (f32[1280]{0:T(1024)S(1)}, f32[1280]{0:T(1024)}, u32[]{:S(2)}) copy-start(f32[1280]{0:T(1024)} %copy-done.20) | copy-start | bytes 15364
  529.7 39.5 %copy-start.23 = (f32[768]{0:T(1024)S(1)}, f32[768]{0:T(1024)}, u32[]{:S(2)}) copy-start(f32[768]{0:T(1024)} %param.26) | copy-start | bytes 9220
  529.7 39.5 %copy-start.38 = (f32[768]{0:T(1024)S(1)}, f32[768]{0:T(1024)}, u32[]{:S(2)}) copy-start(f32[768]{0:T(1024)} %param.27) | copy-start | bytes 9220
  529.7 314.7 %reduce-scatter.16.cloned.1.call-start = ((), (), s32[]{:S(2)}) async-start(), calls=%async_computation.15 | async-start | bytes 2211840
  567.0 1.5 copy-start.15
  576.3 4.8 copy-start.14
  581.0 364.3 %all-gather.12.cloned.1.call-start = ((), (), s32[]{:S(2)}) async-start(), calls=%async_computation.14 | async-start | bytes 19660800 | tf_op jit(solution)/shard_map/all_gather | solution.py:250
  954.3 3.6 copy-start.1
  962.1 6.4 copy-start.25
  962.1 6.4 copy-start.26
  962.1 6.4 copy-start.27
  962.1 6.4 copy-start.28
  962.1 6.4 copy-start.31
  962.1 44.1 %copy-start.8 = (f32[192,768]{1,0:T(8,128)S(1)}, f32[192,768]{1,0:T(8,128)}, u32[]{:S(2)}) copy-start(f32[192,768]{1,0:T(8,128)} %all_gather.42) | copy-start | bytes 1769476
  (5 other events, 5.3 us)
Sparse Core Ops, SparseCore 0:
  52.1 33.0 all-gather.5
  163.2 81.2 all-reduce.4
  275.0 81.3 all-reduce.8
  359.2 49.3 all-reduce.6
  513.3 52.0 reduce-scatter.9
  568.9 62.5 reduce-scatter.17
  634.9 68.1 reduce-scatter.13
  706.6 68.1 reduce-scatter.11
  778.3 66.1 reduce-scatter.15
  846.5 98.8 all-gather.11
Sparse Core Ops, SparseCore 1:
  165.2 30.2 all-gather.7
  196.8 29.4 all-gather.9
